TPU v7x, 512 devices: a whole 4x4x16 slice. The times are simulated.
512 devices in a mesh: dp: 128 (over z, y, core), rep: 4 (over x).
Axes of the slice: x: 4, y: 4, z: 16, core: 2. Of those that a mesh axis runs over, the one named last changes fastest.
Arguments:
- queries: bfloat16 [131072, 1024], P(('dp', 'rep')), may hold values from -24 to 24
- passages: bfloat16 [16384, 1024], P('dp'), may hold values from -24 to 24
- group_topic: int32 [128], replicated, may hold values from 0 to 15
- topic_rows: int32 [16, 1024], replicated, may hold values from 0 to 16383, as said below
- positive: int32 [131072], P(('dp', 'rep')), may hold values from 0 to 1023
Outputs:
- query_loss: float32 [131072], P(('dp', 'rep'))
- query_grad: bfloat16 [131072, 1024], P(('dp', 'rep'))
- passage_grad: bfloat16 [16384, 1024], P('dp')
Inputs may be any that keep to these rules, and one draw needn't show every extreme that they name: `topic_rows`: row t lists the 1024 passages of topic t; its entries k * 8 to (k + 1) * 8 - 1 are passages of rows k * 128 to (k + 1) * 128 - 1; every passage appears exactly once in the table.
All inputs are finite; a program needn't handle non-finite values.
Results may differ from a plain program's by a relative error of at most 0.0046.
Values may be sent and summed in bfloat16 or wider, within the bound.
A program may use at most 64 MiB of HBM per device.

v0:
```python
import jax
import jax.numpy as jnp
from jax import lax
from jax.sharding import PartitionSpec as P

D = 1024
TOPIC_PASS = 1024


def shards(queries, passages, group_topic, topic_rows, positive):
    dp_index = lax.axis_index("dp")
    dp_count = lax.axis_size("dp")
    pass_rows = passages.shape[0]
    width = passages.shape[1]
    topic_count = topic_rows.shape[0]
    per_owner = TOPIC_PASS // dp_count
    columns = lax.dynamic_slice_in_dim(topic_rows, dp_index * per_owner, per_owner, 1)
    selector = (group_topic[:, None] == jnp.arange(topic_count, dtype=jnp.int32)[None, :]).astype(
        jnp.int32
    )
    wanted = jnp.sum(selector[:, :, None] * columns[None, :, :], axis=1) - dp_index * pass_rows
    outgoing = jnp.take(passages, wanted, axis=0)
    gathered = lax.all_to_all(outgoing, "dp", split_axis=0, concat_axis=0, tiled=True)
    picked = gathered.reshape(dp_count * per_owner, width)
    scores = lax.dot_general(
        queries, picked, (((1,), (1,)), ((), ())), preferred_element_type=jnp.float32
    )
    scores = scores * D ** (-0.5)
    top_score = jnp.max(scores, axis=1, keepdims=True)
    lse = top_score + jnp.log(jnp.sum(jnp.exp(scores - top_score), axis=1, keepdims=True))
    onehot = jnp.arange(TOPIC_PASS, dtype=jnp.int32)[None, :] == positive[:, None]
    query_loss = lse[:, 0] - jnp.sum(jnp.where(onehot, scores, jnp.float32(0.0)), axis=1)
    weights = (jnp.exp(scores - lse) - onehot.astype(jnp.float32)).astype(jnp.bfloat16)
    query_grad = jnp.dot(weights, picked, preferred_element_type=jnp.float32).astype(jnp.bfloat16)
    grad_term = lax.dot_general(
        weights, queries, (((0,), (0,)), ((), ())), preferred_element_type=jnp.float32
    )
    grad_term = grad_term.reshape(dp_count, per_owner, width)
    returned = lax.all_to_all(grad_term, "dp", split_axis=0, concat_axis=0, tiled=True)
    dense_rows = jnp.zeros((pass_rows, width), jnp.float32)
    dense_rows = dense_rows.at[wanted.reshape(-1)].add(returned.reshape(-1, width))
    passage_grad = lax.psum(dense_rows, "rep").astype(jnp.bfloat16)
    return (query_loss, query_grad, passage_grad)


def solution(mesh):
    return jax.shard_map(
        shards,
        mesh=mesh,
        in_specs=(P(("dp", "rep"), None), P("dp", None), P(), P(), P(("dp", "rep"))),
        out_specs=(P(("dp", "rep")), P(("dp", "rep"), None), P("dp", None)),
        check_vma=False,
    )
```

profile of v0, /device:TPU:80, one launch (start us, length us, event | category | flops | bytes accessed | tf_op | source)
XLA Modules:
  0.0 360.9 jit_solution(9387834391886115497)
XLA Ops:
  0.6 0.0 copy-start
  0.7 0.7 fusion.21
  1.4 0.8 constant_dynamic-slice_fusion
  2.1 0.1 multiply_reduce_fusion
  2.3 0.1 copy.8
  2.4 0.1 copy.9
  2.5 0.1 reshape.99
  2.6 6.0 %gather_fusion = bf16[1024,1024]{1,0:T(8,128)(2,1)S(1)} fusion(bf16[128,1024]{1,0:T(8,128)(2,1)} %param.6, s32[1024]{0:T(1024)S(1)} %broadcast_clamp_fusion), kind=kCustom, calls=%fused_computation | custom fusion | bytes 4198400 | tf_op jit(solution)/shard_map/jit(_take)/gather | solution.py:22
  8.6 0.3 bitcast_select_fusion
  8.8 116.7 %all_to_all.10 = bf16[128,8,1024]{2,1,0:T(8,128)(2,1)S(1)} all-to-all(bf16[128,8,1024]{2,1,0:T(8,128)(2,1)S(1)} %bitcast_select_fusion), channel_id=1, replica_groups=mesh['dp'=128,'rep'=4] {'dp'}, dimensions={0} | all-to-all | bytes 4194304 | tf_op jit(solution)/shard_map/all_to_all | solution.py:23
  125.5 0.0 copy-done
  125.5 0.0 copy-start.1
  125.5 0.0 copy-start.2
  125.6 0.8 fusion.23
  126.3 0.6 copy-done.1
  126.9 0.0 copy-done.2
  126.9 0.3 fusion.14
  127.2 0.6 fusion.22
  127.8 2.7 convolution_bitcast_fusion
  130.5 9.0 %all-to-all-start.1 = ((f32[128,8,1024]{2,1,0:T(8,128)}), f32[128,8,1024]{2,1,0:T(8,128)}, u32[]{:S(2)}, u32[]{:S(2)}) async-start(f32[128,8,1024]{2,1,0:T(8,128)} %convolution_bitcast_fusion), calls=%async_computation.1 | async-start | bytes 8388608 | tf_op jit(solution)/shard_map/all_to_all | solution.py:39
  139.5 0.1 copy.10
  139.6 0.1 sub.60
  139.7 3.2 fusion.9
  142.9 184.5 %all-to-all-done.1 = f32[128,8,1024]{2,1,0:T(8,128)} async-done(((f32[128,8,1024]{2,1,0:T(8,128)}), f32[128,8,1024]{2,1,0:T(8,128)}, u32[]{:S(2)}, u32[]{:S(2)}) %all-to-all-start.1) | async-done | bytes 4194336 | tf_op jit(solution)/shard_map/all_to_all | solution.py:39
  327.4 10.2 %scatter_custom_fusion = f32[128,1024]{1,0:T(8,128)S(1)} fusion(s32[1024]{0:T(1024)S(1)} %bitcast.43, f32[128,8,1024]{2,1,0:T(8,128)} %all-to-all-done.1, f32[]{:T(128)} %constant.36.clone.1), kind=kCustom, calls=%fused_computation.2 | custom fusion | flops 1048576 | bytes 4718596 | tf_op jit(solution)/shard_map/scatter-add | solution.py:41
  337.5 23.3 %all-reduce.1 = bf16[128,1024]{1,0:T(8,128)(2,1)} all-reduce(f32[128,1024]{1,0:T(8,128)S(1)} %scatter_custom_fusion), channel_id=1, replica_groups=mesh['dp'=128,'rep'=4] {'rep'}, use_global_device_ids=true, to_apply=%region_5.6 | all-reduce | flops 131072 | bytes 786432 | tf_op jit(solution)/shard_map/psum | solution.py:42
  (4 shorter events, 0.0 us)
Async XLA Ops:
  0.6 124.9 %copy-start = (bf16[256,1024]{1,0:T(8,128)(2,1)S(1)}, bf16[256,1024]{1,0:T(8,128)(2,1)}, u32[]{:S(2)}) copy-start(bf16[256,1024]{1,0:T(8,128)(2,1)} %param.5) | copy-start | bytes 1572868
  125.5 1.4 copy-start.1
  125.5 1.4 copy-start.2
  130.5 196.9 %all-to-all-start.1 = ((f32[128,8,1024]{2,1,0:T(8,128)}), f32[128,8,1024]{2,1,0:T(8,128)}, u32[]{:S(2)}, u32[]{:S(2)}) async-start(f32[128,8,1024]{2,1,0:T(8,128)} %convolution_bitcast_fusion), calls=%async_computation.1 | async-start | bytes 8388608 | tf_op jit(solution)/shard_map/all_to_all | solution.py:39
where the time goes:
time: 361 us
  waiting for transfers between devices  184 us (51%)
  blocking collectives  140 us (39%)
  other arithmetic  12.1 us (3%)
  starting transfers between devices  9 us (2%)
  local copies, waits for them, and re-layouts  7.89 us (2%)
  matrix products  6.61 us (2%)
    all_to_all x1, waiting for transfers between devices, shards(): lax.all_to_all(grad_term, 'dp', split_axis=0, concat_axis=0, tiled=True)  184 us
    all_to_all x1, blocking collectives, shards(): lax.all_to_all(outgoing, 'dp', split_axis=0, concat_axis=0, tiled=True)  117 us
    psum x1, blocking collectives, shards(): passage_grad = lax.psum(dense_rows, 'rep').astype(jnp.bfloat16)  23.3 us
    scatter-add x1, other arithmetic, shards(): dense_rows.at[wanted.reshape(-1)].add(returned.reshape(-1, width))  10.2 us
    all_to_all x1, starting transfers between devices, shards(): lax.all_to_all(grad_term, 'dp', split_axis=0, concat_axis=0, tiled=True)  9 us
  transfers between devices with their start and end apart: 1, of which 1 were waited for; matrix products, arithmetic and copies ran while one was open for 1% of the time, Pallas kernels for 0%

commit v1 on v0

v1 whole, which is shorter than its diff:
```python
import jax
import jax.numpy as jnp
from jax import lax
from jax.experimental import pallas as pl
from jax.experimental.pallas import tpu as pltpu
from jax.sharding import PartitionSpec as P

F32, BF16, I32 = jnp.float32, jnp.bfloat16, jnp.int32
MESH = pl.DeviceIdType.MESH
D = 1024
Q = 256
OWN = 128
TOPICS = 16
NZ, NE, NX = 16, 8, 4
SHARE = 2
BLOCK = SHARE * TOPICS
HALF = 128
PARTS = 2
PIECES, PIECE = 4, 32
Q_PACE = (4, 2, 2, 2, 2)
RS_PACE = (4, 4, 4)

STEP = {}
for side in (-1, 1):
    for r in (1, 2, 6, 7):
        STEP[side * r] = side
    for r in (3, 4):
        STEP[side * r] = -side
    STEP[side * 5] = 5 * side
ORDER = (0, -1, 1, -5, 5, -2, 2, -4, 4, -6, 6, -3, 3, -7, 7, 8)
SLOT = {r: n for n, r in enumerate(ORDER)}


def sources(r, i):
    if r == 8:
        return (-1, -7) if i == 0 else (1, 7)
    return STEP[r], r - STEP[r]


CHILDREN = {
    (r, i): [c for c in ORDER if c and sources(c, i)[1] == r] for r in ORDER for i in range(PARTS)
}


def dot(a, b, contract=(1, 0)):
    dims = (((contract[0],), (contract[1],)), ((), ()))
    return lax.dot_general(a, b, dims, preferred_element_type=F32)


def kernel(
    q_ref, p_ref, gt_ref, rows_ref, pos_ref,
    loss_ref, qg_ref, pg_ref,
    loss_v, qg_v, pg_v, pass_here, rows_here, topics, qall, posall, mat, mat_t, smat, smat_t, zbuf, ysend, picked,
    st, part, stats, row, wt,
    gsend, grecv, qpart, rssend, rsrecv, table, bsend, brecv, fin,
    local_sem, q_s, q_r, pos_s, pos_r, z_s, z_r, y_s, y_r,
    stat_s, stat_r, rs_s, rs_r, g_s, g_r, b_s, b_r, fin_s, fin_r,
):
    dp = lax.axis_index("dp")
    x = lax.axis_index("rep")
    z, e = dp // NE, dp % NE
    zs = {d: (lax.rem(z + d + NZ, NZ) * NE + e, x) for d in (-5, -1, 1, 5)}
    x_at = [lax.rem(x + o, NX) for o in range(NX)]
    e_at = [lax.rem(e + o, NE) for o in range(NE)]
    xs = [(dp, x_at[o]) for o in range(NX)]
    es = [(z * NE + e_at[o], x) for o in range(NE)]
    x_up, x_down = xs[1], xs[NX - 1]

    barrier = pltpu.get_barrier_semaphore()
    partners = list(zs.values()) + xs[1:] + es[1:]
    for partner in partners:
        pl.semaphore_signal(barrier, inc=1, device_id=partner, device_id_type=MESH)

    block = pl.ds(pl.multiple_of((dp // 16) * 128, 128), 128)
    loads = [
        pltpu.make_async_copy(src, dst, local_sem.at[n])
        for n, (src, dst) in enumerate(
            (
                (rows_ref.at[:, block], rows_here),
                (p_ref, pass_here),
                (gt_ref, topics),
                (q_ref, qall.at[x]),
                (pos_ref, posall.at[x]),
            )
        )
    ]
    for load in loads:
        load.start()

    started = []

    def send(src, dst, send_sem, recv_sem, to):
        copy = pltpu.make_async_remote_copy(
            src_ref=src, dst_ref=dst, send_sem=send_sem, recv_sem=recv_sem,
            device_id=to, device_id_type=MESH,
        )
        copy.start()
        started.append(copy)
        return copy

    def finish_sends():
        while started:
            started.pop(0).wait_send()

    lane = lax.broadcasted_iota(I32, (TOPICS, OWN), 1)
    first = (dp % 16) * 8
    loads[0].wait()
    here = rows_here[...] - dp * OWN
    for i in range(8):
        col = jnp.sum(jnp.where(lane == first + i, here, 0).astype(F32), axis=1, keepdims=True)
        mat[i * 16 : (i + 1) * 16, :] = jnp.where(lane.astype(F32) == col, 1.0, 0.0).astype(BF16)
    mine = mat[pl.ds(pl.multiple_of(x * BLOCK, BLOCK), BLOCK), :]
    loads[1].wait()
    zbuf[0] = dot(mine, pass_here[...]).astype(BF16)
    for load in loads[2:]:
        load.wait()

    pl.semaphore_wait(barrier, len(partners))

    def sub(i):
        return pl.ds(i * (BLOCK // PARTS), BLOCK // PARTS)

    zc = {}

    def spread(r, i):
        for c in CHILDREN[r, i]:
            n = SLOT[c]
            zc[c, i] = send(
                zbuf.at[SLOT[r], sub(i)], zbuf.at[n, sub(i)],
                z_s.at[n, i], z_r.at[n, i], zs[-sources(c, i)[0]],
            )

    for i in range(PARTS):
        spread(0, i)

    qc, seen = {}, set()

    def got(copies, *keys):
        for key in keys:
            if (id(copies), key) not in seen:
                seen.add((id(copies), key))
                copies[key].wait_recv()

    def send_q(way, n):
        stage, i = divmod(n, PIECES)
        half = way if stage != 1 else 1 - way
        owner = x
        if stage == 2:
            owner = x_at[1] if way else x_at[3]
            got(qc, (way, i))
        rows = qall.at[owner, pl.ds(half * HALF + i * PIECE, PIECE)]
        qc[way, n] = send(rows, rows, q_s.at[way, n], q_r.at[way, n], x_down if way else x_up)

    def paced(send_piece, pace, h):
        for n in range(sum(pace[:h]), sum(pace[: h + 1])):
            send_piece(0, n)
            send_piece(1, n)

    paced(send_q, Q_PACE, 0)

    r16 = lax.broadcasted_iota(I32, (16, 256), 0)
    c256 = lax.broadcasted_iota(I32, (16, 256), 1)
    at = (r16 // 2) * BLOCK + (r16 % 2) * TOPICS
    for d in range(NE):
        chosen = at + topics[z * NE + d]
        smat[d * 16 : (d + 1) * 16, :] = jnp.where(c256 == chosen, 1.0, 0.0).astype(BF16)
    smat_t[...] = smat[...].T
    mat_t[...] = mat[...].T

    yc = {}

    def pick(ch):
        blocks = zbuf[ch * 8 : (ch + 1) * 8].reshape(256, D)
        ysend[ch] = dot(smat[...], blocks).astype(BF16).reshape(NE, 16, D)
        for o in range(1, NE):
            yc[ch, o] = send(
                ysend.at[ch, e_at[o]], picked.at[ch, e],
                y_s.at[ch, o - 1], y_r.at[ch, o - 1], es[o],
            )
        picked[ch, e] = ysend[ch, e]

    def receive(*distances):
        for i in range(PARTS):
            for r in distances:
                zc[r, i].wait_recv()
                spread(r, i)

    receive(-1, 1)
    paced(send_q, Q_PACE, 1)
    pos_c = [
        send(posall.at[x], posall.at[x], pos_s.at[o - 1], pos_r.at[o - 1], xs[o])
        for o in range(1, NX)
    ]
    receive(-5, 5)
    paced(send_q, Q_PACE, 2)
    receive(-2, 2, -4, 4, -6, 6)
    paced(send_q, Q_PACE, 3)
    pick(0)
    paced(send_q, Q_PACE, 4)
    receive(-3, 3, -7, 7)
    receive(8)
    pick(1)

    p = lax.broadcasted_iota(I32, (128, 1), 0)
    listed_at = []
    for ch in range(2):
        away = jnp.zeros((128, 1), I32)
        for n in range(8):
            away = jnp.where((p // 2) % 8 == n, ORDER[ch * 8 + n], away)
        z_of = (z + away + NZ) % NZ
        listed_at.append(z_of * 64 + (p // 16) * 8 + x * SHARE + p % 2)

    def columns(n):
        return pl.ds(pl.multiple_of(n * Q, Q), Q)

    def score(ch, n):
        cols = columns(n)
        s = dot(picked[ch].reshape(128, D), qall[n], (1, 1)) * (D ** -0.5)
        st[ch, :, cols] = s
        top = jnp.max(s, axis=0, keepdims=True)
        part[ch, 0:1, cols] = top
        part[ch, 1:2, cols] = jnp.sum(jnp.exp(s - top), axis=0, keepdims=True)
        hot = listed_at[ch] == posall[n]
        part[ch, 2:3, cols] = jnp.sum(jnp.where(hot, s, 0.0), axis=0, keepdims=True)

    for copy in pos_c:
        copy.wait_recv()
    for o in range(1, NE):
        yc[0, o].wait_recv()
    score(0, x_at[0])
    got(qc, *((0, n) for n in range(2 * PIECES)))
    score(0, x_at[3])
    got(qc, *((1, n) for n in range(2 * PIECES)))
    score(0, x_at[1])
    for o in range(1, NE):
        yc[1, o].wait_recv()
    for o in (0, 3, 1):
        score(1, x_at[o])
    got(qc, *((way, n) for way in range(2) for n in range(2 * PIECES, 3 * PIECES)))
    score(0, x_at[2])
    score(1, x_at[2])

    def merge(pieces):
        top = pieces[0][0]
        for piece in pieces[1:]:
            top = jnp.maximum(top, piece[0])
        total = sum(piece[1] * jnp.exp(piece[0] - top) for piece in pieces)
        return top, total, sum(piece[2] for piece in pieces)

    def rows_of(ref, n):
        return ref[n, 0:1, :], ref[n, 1:2, :], ref[n, 2:3, :]

    top, total, hit = merge([rows_of(part, ch) for ch in range(2)])
    r8 = lax.broadcasted_iota(I32, (8, NX * Q), 0)
    stats[x] = jnp.where(r8 == 0, top, jnp.where(r8 == 1, total, hit))
    finish_fwd = list(started)
    started.clear()
    stat_c = [
        send(stats.at[x], stats.at[x], stat_s.at[o - 1], stat_r.at[o - 1], xs[o])
        for o in range(1, NX)
    ]
    for copy in finish_fwd:
        copy.wait_send()
    for copy in stat_c:
        copy.wait_recv()
    top, total, hit = merge([rows_of(stats, n) for n in range(NX)])
    lse = top + jnp.log(total)
    row[0:1, :] = lse
    row[1:2, :] = lse - hit
    loss_v[...] = row[1:2, columns(x)]
    stores = [pltpu.make_async_copy(loss_v.at[0], loss_ref, local_sem.at[5])]
    stores[0].start()

    for ch in range(2):
        for n in range(NX):
            cols = pl.ds(n * Q, Q)
            hot = jnp.where(listed_at[ch] == posall[n], 1.0, 0.0)
            w = jnp.exp(st[ch, :, cols] - row[0:1, cols]) - hot
            wt[ch * 128 : (ch + 1) * 128, cols] = w.astype(BF16)

    def term(n, _):
        cols = pl.ds(pl.multiple_of(n * 256, 256), 256)
        g = dot(wt[...], qall[:, :, cols].reshape(NX * Q, 256))
        gsend[:, :, :, cols] = g.astype(BF16).reshape(2, NE, 16, 256)
        return 0

    lax.fori_loop(0, D // 256, term, 0)
    gc = {}
    for c in (1, 0):
        for o in range(1, NE):
            gc[c, o] = send(
                gsend.at[c, e_at[o]], grecv.at[c, e],
                g_s.at[c, o - 1], g_r.at[c, o - 1], es[o],
            )
        grecv[c, e] = gsend[c, e]

    def query_part(o):
        w = wt[:, columns(x_at[o])].T

        def tile(n, _):
            out = pl.ds(pl.multiple_of(n * 256, 256), 256)
            qpart[o, :, out] = dot(w, picked[:, :, :, out].reshape(256, 256))
            return 0

        lax.fori_loop(0, D // 256, tile, 0)

    rs = {}

    def send_rs(way, n):
        stage, i = divmod(n, PIECES)
        half = way if stage == 1 else 1 - way
        rows = pl.ds(i * PIECE, PIECE)
        value = qpart[2 if stage == 0 else 3 if way else 1, pl.ds(half * HALF + i * PIECE, PIECE)]
        if stage == 2:
            got(rs, (way, i))
            value = value + rsrecv[way, 0, rows].astype(F32)
        rssend[way, stage, rows] = value.astype(BF16)
        rs[way, n] = send(
            rssend.at[way, stage, rows], rsrecv.at[way, stage, rows],
            rs_s.at[way, n], rs_r.at[way, n], x_down if way else x_up,
        )

    query_part(2)
    paced(send_rs, RS_PACE, 0)
    query_part(1)
    query_part(3)

    def sum_by_topic(c):
        for o in range(1, NE):
            gc[c, o].wait_recv()
        sums = dot(smat_t[...], grecv[c].reshape(128, D))
        table[c * 8 : (c + 1) * 8] = sums.reshape(8, BLOCK, D)

    paced(send_rs, RS_PACE, 1)
    sum_by_topic(1)
    bc = {}

    def summed(r, i):
        value = table[SLOT[r], sub(i)]
        for c in CHILDREN[r, i]:
            bc[c, i].wait_recv()
            value = value + brecv[SLOT[c], sub(i)].astype(F32)
        return value.astype(BF16)

    def send_back(*distances):
        for i in range(PARTS):
            for r in distances:
                n = SLOT[r]
                bsend[n, sub(i)] = summed(r, i)
                bc[r, i] = send(
                    bsend.at[n, sub(i)], brecv.at[n, sub(i)],
                    b_s.at[n, i], b_r.at[n, i], zs[sources(r, i)[0]],
                )

    send_back(8, -3, 3)
    sum_by_topic(0)
    send_back(-7, 7)
    send_back(-4, 4, -2, 2, -6, 6)
    paced(send_rs, RS_PACE, 2)
    send_back(-5, 5, -1, 1)
    fin_c = []
    for i in range(PARTS):
        fin[x, sub(i)] = summed(0, i)
        for o in range(1, NX):
            rows = fin.at[x, sub(i)]
            fin_c.append(send(rows, rows, fin_s.at[o - 1, i], fin_r.at[o - 1, i], xs[o]))
    query_part(0)
    got(rs, *((way, n) for n in range(PIECES, 3 * PIECES) for way in range(2)))
    for half in range(2):
        rows = pl.ds(half * HALF, HALF)
        value = qpart[0, rows] + rsrecv[half, 1].astype(F32) + rsrecv[1 - half, 2].astype(F32)
        qg_v[rows] = value.astype(BF16)
    stores.append(pltpu.make_async_copy(qg_v, qg_ref, local_sem.at[6]))
    stores[1].start()
    for copy in fin_c:
        copy.wait_recv()
    pg_v[...] = dot(mat_t[...], fin[...].reshape(OWN, D)).astype(BF16)
    stores.append(pltpu.make_async_copy(pg_v, pg_ref, local_sem.at[7]))
    stores[2].start()
    finish_sends()
    for store in stores:
        store.wait()


def shards(queries, passages, group_topic, topic_rows, positive):
    hbm = pl.BlockSpec(memory_space=pltpu.HBM)
    dma = pltpu.SemaphoreType.DMA
    loss, query_grad, passage_grad = pl.pallas_call(
        kernel,
        out_shape=(
            jax.ShapeDtypeStruct((Q,), F32),
            jax.ShapeDtypeStruct((Q, D), BF16),
            jax.ShapeDtypeStruct((OWN, D), BF16),
        ),
        in_specs=[hbm] * 5,
        out_specs=(hbm, hbm, hbm),
        scratch_shapes=[
            pltpu.VMEM((1, Q), F32),
            pltpu.VMEM((Q, D), BF16),
            pltpu.VMEM((OWN, D), BF16),
            pltpu.VMEM((OWN, D), BF16),
            pltpu.VMEM((TOPICS, 128), I32),
            pltpu.SMEM((128,), I32),
            pltpu.VMEM((NX, Q, D), BF16),
            pltpu.VMEM((NX, 1, Q), I32),
            pltpu.VMEM((OWN, OWN), BF16),
            pltpu.VMEM((OWN, OWN), BF16),
            pltpu.VMEM((128, 256), BF16),
            pltpu.VMEM((256, 128), BF16),
            pltpu.VMEM((NZ, BLOCK, D), BF16),
            pltpu.VMEM((2, NE, 16, D), BF16),
            pltpu.VMEM((2, NE, 16, D), BF16),
            pltpu.VMEM((2, 128, NX * Q), F32),
            pltpu.VMEM((2, 8, NX * Q), F32),
            pltpu.VMEM((NX, 8, NX * Q), F32),
            pltpu.VMEM((8, NX * Q), F32),
            pltpu.VMEM((256, NX * Q), BF16),
            pltpu.VMEM((2, NE, 16, D), BF16),
            pltpu.VMEM((2, NE, 16, D), BF16),
            pltpu.VMEM((NX, Q, D), F32),
            pltpu.VMEM((2, 3, HALF, D), BF16),
            pltpu.VMEM((2, 3, HALF, D), BF16),
            pltpu.VMEM((NZ, BLOCK, D), F32),
            pltpu.VMEM((NZ, BLOCK, D), BF16),
            pltpu.VMEM((NZ, BLOCK, D), BF16),
            pltpu.VMEM((NX, BLOCK, D), BF16),
            dma((8,)),
            dma((2, 3 * PIECES)), dma((2, 3 * PIECES)), dma((3,)), dma((3,)),
            dma((NZ, PARTS)), dma((NZ, PARTS)),
            dma((2, NE - 1)), dma((2, NE - 1)),
            dma((3,)), dma((3,)), dma((2, 3 * PIECES)), dma((2, 3 * PIECES)),
            dma((2, NE - 1)), dma((2, NE - 1)),
            dma((NZ, PARTS)), dma((NZ, PARTS)),
            dma((3, PARTS)), dma((3, PARTS)),
        ],
        compiler_params=pltpu.CompilerParams(
            collective_id=0, has_side_effects=True, vmem_limit_bytes=60 * 1024 * 1024
        ),
        cost_estimate=pl.CostEstimate(
            flops=3 * 2 * 256 * 1024 * 1024, bytes_accessed=2 * 1024 * 1024, transcendentals=2 * 256 * 1024
        ),
    )(queries, passages, group_topic, topic_rows, positive.reshape(1, Q))
    return loss, query_grad, passage_grad


def solution(mesh):
    return jax.shard_map(
        shards,
        mesh=mesh,
        in_specs=(P(("dp", "rep"), None), P("dp", None), P(), P(), P(("dp", "rep"))),
        out_specs=(P(("dp", "rep")), P(("dp", "rep"), None), P("dp", None)),
        check_vma=False,
    )
```

time: 361 us -> 87.7 us (0.24)
  the two profiles are of different devices: /device:TPU:80 before, /device:TPU:64 now
where the time goes in v1:
time: 87.7 us; the launch traced here: 87.5 us
  Pallas kernels  83 us (95%)
  local copies, waits for them, and re-layouts  3.84 us (4%)
    pallas_call x1, Pallas kernels, shards(): pl.pallas_call(kernel, out_shape=(jax.ShapeDtypeStruct((Q,), F32), jax.Sh...  83 us
    unnamed x7, local copies, waits for them, and re-layouts  3.84 us

profile of v1, /device:TPU:64, one launch (start us, length us, event | category | flops | bytes accessed | tf_op | source)
XLA Modules:
  0.0 87.5 jit_solution(902526242524829395)
XLA Ops:
  0.6 83.0 %shard_map.76 = (f32[256]{0:T(256)}, bf16[256,1024]{1,0:T(8,128)(2,1)}, bf16[128,1024]{1,0:T(8,128)(2,1)}) custom-call(bf16[256,1024]{1,0:T(8,128)(2,1)} %q_ref.1, bf16[128,1024]{1,0:T(8,128)(2,1)} %p_ref.1, s32[128]{0:T(128)} %gt_ref.1, s32[16,1024]{1,0:T(8,128)} %rows_ref.1, s32[1,256]{1,0:T(1,128)} %bitcast.1), custom_call_target="tpu_custom_call" | custom-call | flops 1610612736 | bytes 2097152 | tf_op jit(solution)/shard_map/pallas_call | solution.py:388
  83.7 0.0 copy-start.1
  83.7 0.7 copy-done.1
  84.3 0.6 copy.11
  84.9 0.0 copy-start
  84.9 1.9 %copy.12 = bf16[256,1024]{1,0:T(8,128)(2,1)} copy(bf16[256,1024]{1,0:T(8,128)(2,1)} %get-tuple-element.7) | data formatting | bytes 1048576
  86.8 0.0 copy-done
  86.8 0.7 copy.13
Async XLA Ops:
  83.7 0.7 copy-start.1
  84.9 1.9 %copy-start = (bf16[128,1024]{1,0:T(8,128)(2,1)S(1)}, bf16[128,1024]{1,0:T(8,128)(2,1)}, u32[]{:S(2)}) copy-start(bf16[128,1024]{1,0:T(8,128)(2,1)} %get-tuple-element.8) | copy-start | bytes 786436

commit v2 on v1

--- a/solution.py
+++ b/solution.py
@@ -15,7 +15,7 @@
 SHARE = 2
 BLOCK = SHARE * TOPICS
 HALF = 128
-PARTS = 2
+PARTS = 4
 PIECES, PIECE = 4, 32
 Q_PACE = (4, 2, 2, 2, 2)
 RS_PACE = (4, 4, 4)
@@ -33,7 +33,7 @@
 
 def sources(r, i):
     if r == 8:
-        return (-1, -7) if i == 0 else (1, 7)
+        return (-1, -7) if i < PARTS // 2 else (1, 7)
     return STEP[r], r - STEP[r]
 
 
@@ -117,8 +117,8 @@
 
     pl.semaphore_wait(barrier, len(partners))
 
-    def sub(i):
-        return pl.ds(i * (BLOCK // PARTS), BLOCK // PARTS)
+    def sub(n, i):
+        return n, pl.ds(i // 2 * 16, 16), pl.ds(i % 2 * 512, 512)
 
     zc = {}
 
@@ -126,7 +126,7 @@
         for c in CHILDREN[r, i]:
             n = SLOT[c]
             zc[c, i] = send(
-                zbuf.at[SLOT[r], sub(i)], zbuf.at[n, sub(i)],
+                zbuf.at[sub(SLOT[r], i)], zbuf.at[sub(n, i)],
                 z_s.at[n, i], z_r.at[n, i], zs[-sources(c, i)[0]],
             )
 
@@ -218,10 +218,12 @@
         s = dot(picked[ch].reshape(128, D), qall[n], (1, 1)) * (D ** -0.5)
         st[ch, :, cols] = s
         top = jnp.max(s, axis=0, keepdims=True)
-        part[ch, 0:1, cols] = top
-        part[ch, 1:2, cols] = jnp.sum(jnp.exp(s - top), axis=0, keepdims=True)
+        total = jnp.sum(jnp.exp(s - top), axis=0, keepdims=True)
         hot = listed_at[ch] == posall[n]
-        part[ch, 2:3, cols] = jnp.sum(jnp.where(hot, s, 0.0), axis=0, keepdims=True)
+        hit = jnp.sum(jnp.where(hot, s, 0.0), axis=0, keepdims=True)
+        for k, value in enumerate((top, total, hit)):
+            for h in range(2):
+                part[ch, k, pl.ds(n * 2 + h, 1), :] = value[:, h * 128 : (h + 1) * 128]
 
     for copy in pos_c:
         copy.wait_recv()
@@ -247,12 +249,11 @@
         total = sum(piece[1] * jnp.exp(piece[0] - top) for piece in pieces)
         return top, total, sum(piece[2] for piece in pieces)
 
-    def rows_of(ref, n):
-        return ref[n, 0:1, :], ref[n, 1:2, :], ref[n, 2:3, :]
-
-    top, total, hit = merge([rows_of(part, ch) for ch in range(2)])
-    r8 = lax.broadcasted_iota(I32, (8, NX * Q), 0)
-    stats[x] = jnp.where(r8 == 0, top, jnp.where(r8 == 1, total, hit))
+    def pieces_of(ref, count):
+        return [[ref[n, k] for k in range(3)] for n in range(count)]
+
+    for k, value in enumerate(merge(pieces_of(part, 2))):
+        stats[x, k] = value
     finish_fwd = list(started)
     started.clear()
     stat_c = [
@@ -263,39 +264,38 @@
         copy.wait_send()
     for copy in stat_c:
         copy.wait_recv()
-    top, total, hit = merge([rows_of(stats, n) for n in range(NX)])
+    top, total, hit = merge(pieces_of(stats, NX))
     lse = top + jnp.log(total)
-    row[0:1, :] = lse
-    row[1:2, :] = lse - hit
-    loss_v[...] = row[1:2, columns(x)]
-    stores = [pltpu.make_async_copy(loss_v.at[0], loss_ref, local_sem.at[5])]
+    row[0] = lse
+    row[1] = lse - hit
+    loss_v[...] = row[1, pl.ds(x * 2, 2), :]
+    stores = [pltpu.make_async_copy(loss_v, loss_ref, local_sem.at[5])]
     stores[0].start()
 
-    for ch in range(2):
+    gc = {}
+    for ch in (1, 0):
         for n in range(NX):
             cols = pl.ds(n * Q, Q)
             hot = jnp.where(listed_at[ch] == posall[n], 1.0, 0.0)
-            w = jnp.exp(st[ch, :, cols] - row[0:1, cols]) - hot
-            wt[ch * 128 : (ch + 1) * 128, cols] = w.astype(BF16)
-
-    def term(n, _):
-        cols = pl.ds(pl.multiple_of(n * 256, 256), 256)
-        g = dot(wt[...], qall[:, :, cols].reshape(NX * Q, 256))
-        gsend[:, :, :, cols] = g.astype(BF16).reshape(2, NE, 16, 256)
-        return 0
-
-    lax.fori_loop(0, D // 256, term, 0)
-    gc = {}
-    for c in (1, 0):
+            lse = jnp.concatenate([row[0, 2 * n : 2 * n + 1, :], row[0, 2 * n + 1 : 2 * n + 2, :]], axis=1)
+            wt[ch, :, cols] = (jnp.exp(st[ch, :, cols] - lse) - hot).astype(BF16)
+
+        def term(n, _):
+            cols = pl.ds(pl.multiple_of(n * 256, 256), 256)
+            g = dot(wt[ch], qall[:, :, cols].reshape(NX * Q, 256))
+            gsend[ch, :, :, cols] = g.astype(BF16).reshape(NE, 16, 256)
+            return 0
+
+        lax.fori_loop(0, D // 256, term, 0)
         for o in range(1, NE):
-            gc[c, o] = send(
-                gsend.at[c, e_at[o]], grecv.at[c, e],
-                g_s.at[c, o - 1], g_r.at[c, o - 1], es[o],
+            gc[ch, o] = send(
+                gsend.at[ch, e_at[o]], grecv.at[ch, e],
+                g_s.at[ch, o - 1], g_r.at[ch, o - 1], es[o],
             )
-        grecv[c, e] = gsend[c, e]
+        grecv[ch, e] = gsend[ch, e]
 
     def query_part(o):
-        w = wt[:, columns(x_at[o])].T
+        w = wt[:, :, columns(x_at[o])].reshape(256, Q).T
 
         def tile(n, _):
             out = pl.ds(pl.multiple_of(n * 256, 256), 256)
@@ -336,19 +336,19 @@
     bc = {}
 
     def summed(r, i):
-        value = table[SLOT[r], sub(i)]
+        value = table[sub(SLOT[r], i)]
         for c in CHILDREN[r, i]:
             bc[c, i].wait_recv()
-            value = value + brecv[SLOT[c], sub(i)].astype(F32)
+            value = value + brecv[sub(SLOT[c], i)].astype(F32)
         return value.astype(BF16)
 
     def send_back(*distances):
         for i in range(PARTS):
             for r in distances:
                 n = SLOT[r]
-                bsend[n, sub(i)] = summed(r, i)
+                bsend[sub(n, i)] = summed(r, i)
                 bc[r, i] = send(
-                    bsend.at[n, sub(i)], brecv.at[n, sub(i)],
+                    bsend.at[sub(n, i)], brecv.at[sub(n, i)],
                     b_s.at[n, i], b_r.at[n, i], zs[sources(r, i)[0]],
                 )
 
@@ -360,9 +360,9 @@
     send_back(-5, 5, -1, 1)
     fin_c = []
     for i in range(PARTS):
-        fin[x, sub(i)] = summed(0, i)
+        fin[sub(x, i)] = summed(0, i)
         for o in range(1, NX):
-            rows = fin.at[x, sub(i)]
+            rows = fin.at[sub(x, i)]
             fin_c.append(send(rows, rows, fin_s.at[o - 1, i], fin_r.at[o - 1, i], xs[o]))
     query_part(0)
     got(rs, *((way, n) for n in range(PIECES, 3 * PIECES) for way in range(2)))
@@ -388,14 +388,14 @@
     loss, query_grad, passage_grad = pl.pallas_call(
         kernel,
         out_shape=(
-            jax.ShapeDtypeStruct((Q,), F32),
+            jax.ShapeDtypeStruct((2, 128), F32),
             jax.ShapeDtypeStruct((Q, D), BF16),
             jax.ShapeDtypeStruct((OWN, D), BF16),
         ),
         in_specs=[hbm] * 5,
         out_specs=(hbm, hbm, hbm),
         scratch_shapes=[
-            pltpu.VMEM((1, Q), F32),
+            pltpu.VMEM((2, 128), F32),
             pltpu.VMEM((Q, D), BF16),
             pltpu.VMEM((OWN, D), BF16),
             pltpu.VMEM((OWN, D), BF16),
@@ -411,10 +411,10 @@
             pltpu.VMEM((2, NE, 16, D), BF16),
             pltpu.VMEM((2, NE, 16, D), BF16),
             pltpu.VMEM((2, 128, NX * Q), F32),
-            pltpu.VMEM((2, 8, NX * Q), F32),
-            pltpu.VMEM((NX, 8, NX * Q), F32),
-            pltpu.VMEM((8, NX * Q), F32),
-            pltpu.VMEM((256, NX * Q), BF16),
+            pltpu.VMEM((2, 3, 8, 128), F32),
+            pltpu.VMEM((NX, 3, 8, 128), F32),
+            pltpu.VMEM((2, 8, 128), F32),
+            pltpu.VMEM((2, 128, NX * Q), BF16),
             pltpu.VMEM((2, NE, 16, D), BF16),
             pltpu.VMEM((2, NE, 16, D), BF16),
             pltpu.VMEM((NX, Q, D), F32),
@@ -440,7 +440,7 @@
             flops=3 * 2 * 256 * 1024 * 1024, bytes_accessed=2 * 1024 * 1024, transcendentals=2 * 256 * 1024
         ),
     )(queries, passages, group_topic, topic_rows, positive.reshape(1, Q))
-    return loss, query_grad, passage_grad
+    return loss.reshape(Q), query_grad, passage_grad
 
 
 def solution(mesh):

time: 87.7 us -> 87.1 us (level)
  the two profiles are of different devices: /device:TPU:64 before, /device:TPU:2 now
where the time goes in v2:
time: 87.1 us; the launch traced here: 87 us
  Pallas kernels  82.5 us (95%)
  local copies, waits for them, and re-layouts  3.84 us (4%)
    pallas_call x1, Pallas kernels, shards(): pl.pallas_call(kernel, out_shape=(jax.ShapeDtypeStruct((2, 128), F32), ja...  82.5 us
    unnamed x7, local copies, waits for them, and re-layouts  3.84 us

profile of v2, /device:TPU:2, one launch (start us, length us, event | category | flops | bytes accessed | tf_op | source)
XLA Modules:
  0.0 87.0 jit_solution(680417046234317308)
XLA Ops:
  0.6 82.5 %shard_map.76 = (f32[2,128]{1,0:T(2,128)}, bf16[256,1024]{1,0:T(8,128)(2,1)}, bf16[128,1024]{1,0:T(8,128)(2,1)}) custom-call(bf16[256,1024]{1,0:T(8,128)(2,1)} %q_ref.1, bf16[128,1024]{1,0:T(8,128)(2,1)} %p_ref.1, s32[128]{0:T(128)} %gt_ref.1, s32[16,1024]{1,0:T(8,128)} %rows_ref.1, s32[1,256]{1,0:T(1,128)} %bitcast.3), custom_call_target="tpu_custom_call" | custom-call | flops 1610612736 | bytes 2097152 | tf_op jit(solution)/shard_map/pallas_call | solution.py:388
  83.1 0.0 copy-start.1
  83.1 0.7 copy-done.1
  83.8 0.6 copy.11
  84.3 0.0 copy-start
  84.3 1.9 %copy.12 = bf16[256,1024]{1,0:T(8,128)(2,1)} copy(bf16[256,1024]{1,0:T(8,128)(2,1)} %get-tuple-element.13) | data formatting | bytes 1048576
  86.3 0.0 copy-done
  86.3 0.7 copy.13
Async XLA Ops:
  83.1 0.7 copy-start.1
  84.3 1.9 %copy-start = (bf16[128,1024]{1,0:T(8,128)(2,1)S(1)}, bf16[128,1024]{1,0:T(8,128)(2,1)}, u32[]{:S(2)}) copy-start(bf16[128,1024]{1,0:T(8,128)(2,1)} %get-tuple-element.14) | copy-start | bytes 786436

commit v3 on v2

--- a/solution.py
+++ b/solution.py
@@ -15,31 +15,21 @@
 SHARE = 2
 BLOCK = SHARE * TOPICS
 HALF = 128
-PARTS = 4
-PIECES, PIECE = 4, 32
-Q_PACE = (4, 2, 2, 2, 2)
-RS_PACE = (4, 4, 4)
-
-STEP = {}
-for side in (-1, 1):
-    for r in (1, 2, 6, 7):
-        STEP[side * r] = side
-    for r in (3, 4):
-        STEP[side * r] = -side
-    STEP[side * 5] = 5 * side
-ORDER = (0, -1, 1, -5, 5, -2, 2, -4, 4, -6, 6, -3, 3, -7, 7, 8)
-SLOT = {r: n for n, r in enumerate(ORDER)}
-
-
-def sources(r, i):
-    if r == 8:
-        return (-1, -7) if i < PARTS // 2 else (1, 7)
-    return STEP[r], r - STEP[r]
-
-
-CHILDREN = {
-    (r, i): [c for c in ORDER if c and sources(c, i)[1] == r] for r in ORDER for i in range(PARTS)
-}
+PARTS = 2
+Q_PACE = (1, 1, 1)
+PIECES, PIECE = 1, 128
+
+ORDER = (0, -1, -5, 5, 1, -2, -6, 4, -4, 6, 2, -7, 3, -3, 7, 8)
+STEPS = (
+    ((0, 2, 1, 5), (0, 3, 1, -5), (0, 1, 1, 1), (0, 4, 1, -1)),
+    ((1, 5, 3, 1), (2, 8, 3, -1)),
+    ((6, 11, 2, 1), (8, 13, 2, -1)),
+    ((11, 15, 1, 1), (14, 15, 1, -1)),
+)
+
+
+def parts_of(step, m):
+    return (m,) if step == 3 else tuple(range(PARTS))
 
 
 def dot(a, b, contract=(1, 0)):
@@ -117,18 +107,18 @@
 
     pl.semaphore_wait(barrier, len(partners))
 
-    def sub(n, i):
-        return n, pl.ds(i // 2 * 16, 16), pl.ds(i % 2 * 512, 512)
+    def sub(first, count, i):
+        return pl.ds(first, count), pl.ds(i * 16, 16)
 
     zc = {}
 
-    def spread(r, i):
-        for c in CHILDREN[r, i]:
-            n = SLOT[c]
-            zc[c, i] = send(
-                zbuf.at[sub(SLOT[r], i)], zbuf.at[sub(n, i)],
-                z_s.at[n, i], z_r.at[n, i], zs[-sources(c, i)[0]],
-            )
+    def spread(step, i):
+        for m, (src, dst, count, far) in enumerate(STEPS[step]):
+            if i in parts_of(step, m):
+                zc[step, m, i] = send(
+                    zbuf.at[sub(src, count, i)], zbuf.at[sub(dst, count, i)],
+                    z_s.at[dst, i], z_r.at[dst, i], zs[far],
+                )
 
     for i in range(PARTS):
         spread(0, i)
@@ -179,26 +169,25 @@
             )
         picked[ch, e] = ysend[ch, e]
 
-    def receive(*distances):
+    def receive(step):
         for i in range(PARTS):
-            for r in distances:
-                zc[r, i].wait_recv()
-                spread(r, i)
-
-    receive(-1, 1)
+            for m in range(len(STEPS[step])):
+                if i in parts_of(step, m):
+                    zc[step, m, i].wait_recv()
+            if step < 3:
+                spread(step + 1, i)
+
+    receive(0)
     paced(send_q, Q_PACE, 1)
     pos_c = [
         send(posall.at[x], posall.at[x], pos_s.at[o - 1], pos_r.at[o - 1], xs[o])
         for o in range(1, NX)
     ]
-    receive(-5, 5)
+    receive(1)
     paced(send_q, Q_PACE, 2)
-    receive(-2, 2, -4, 4, -6, 6)
-    paced(send_q, Q_PACE, 3)
     pick(0)
-    paced(send_q, Q_PACE, 4)
-    receive(-3, 3, -7, 7)
-    receive(8)
+    receive(2)
+    receive(3)
     pick(1)
 
     p = lax.broadcasted_iota(I32, (128, 1), 0)
@@ -272,21 +261,23 @@
     stores = [pltpu.make_async_copy(loss_v, loss_ref, local_sem.at[5])]
     stores[0].start()
 
-    gc = {}
-    for ch in (1, 0):
+    gc, rs = {}, {}
+
+    def weigh(ch):
         for n in range(NX):
             cols = pl.ds(n * Q, Q)
             hot = jnp.where(listed_at[ch] == posall[n], 1.0, 0.0)
             lse = jnp.concatenate([row[0, 2 * n : 2 * n + 1, :], row[0, 2 * n + 1 : 2 * n + 2, :]], axis=1)
             wt[ch, :, cols] = (jnp.exp(st[ch, :, cols] - lse) - hot).astype(BF16)
 
-        def term(n, _):
+    def term(ch):
+        def tile(n, _):
             cols = pl.ds(pl.multiple_of(n * 256, 256), 256)
             g = dot(wt[ch], qall[:, :, cols].reshape(NX * Q, 256))
             gsend[ch, :, :, cols] = g.astype(BF16).reshape(NE, 16, 256)
             return 0
 
-        lax.fori_loop(0, D // 256, term, 0)
+        lax.fori_loop(0, D // 256, tile, 0)
         for o in range(1, NE):
             gc[ch, o] = send(
                 gsend.at[ch, e_at[o]], grecv.at[ch, e],
@@ -304,26 +295,32 @@
 
         lax.fori_loop(0, D // 256, tile, 0)
 
-    rs = {}
-
-    def send_rs(way, n):
-        stage, i = divmod(n, PIECES)
-        half = way if stage == 1 else 1 - way
-        rows = pl.ds(i * PIECE, PIECE)
-        value = qpart[2 if stage == 0 else 3 if way else 1, pl.ds(half * HALF + i * PIECE, PIECE)]
-        if stage == 2:
-            got(rs, (way, i))
-            value = value + rsrecv[way, 0, rows].astype(F32)
-        rssend[way, stage, rows] = value.astype(BF16)
-        rs[way, n] = send(
-            rssend.at[way, stage, rows], rsrecv.at[way, stage, rows],
-            rs_s.at[way, n], rs_r.at[way, n], x_down if way else x_up,
-        )
-
+    def send_rs(way, stage):
+        for i in range(PIECES):
+            half = way if stage == 1 else 1 - way
+            rows = pl.ds(i * PIECE, PIECE)
+            value = qpart[2 if stage == 0 else 3 if way else 1, pl.ds(half * HALF + i * PIECE, PIECE)]
+            n = stage * PIECES + i
+            if stage == 2:
+                got(rs, (way, i))
+                value = value + rsrecv[way, 0, rows].astype(F32)
+            rssend[way, stage, rows] = value.astype(BF16)
+            rs[way, n] = send(
+                rssend.at[way, stage, rows], rsrecv.at[way, stage, rows],
+                rs_s.at[way, n], rs_r.at[way, n], x_down if way else x_up,
+            )
+
+    weigh(1)
+    term(1)
+    weigh(0)
     query_part(2)
-    paced(send_rs, RS_PACE, 0)
+    send_rs(0, 0)
+    send_rs(1, 0)
     query_part(1)
+    send_rs(0, 1)
     query_part(3)
+    send_rs(1, 1)
+    term(0)
 
     def sum_by_topic(c):
         for o in range(1, NE):
@@ -331,39 +328,52 @@
         sums = dot(smat_t[...], grecv[c].reshape(128, D))
         table[c * 8 : (c + 1) * 8] = sums.reshape(8, BLOCK, D)
 
-    paced(send_rs, RS_PACE, 1)
     sum_by_topic(1)
     bc = {}
 
-    def summed(r, i):
-        value = table[sub(SLOT[r], i)]
-        for c in CHILDREN[r, i]:
-            bc[c, i].wait_recv()
-            value = value + brecv[sub(SLOT[c], i)].astype(F32)
-        return value.astype(BF16)
-
-    def send_back(*distances):
+    def summed(first, count, i):
+        values = [table[first + n, sub(0, 1, i)[1]] for n in range(count)]
+        for step in range(1, 4):
+            for m, (src, dst, width, _) in enumerate(STEPS[step]):
+                held = [n for n in range(width) if first <= src + n < first + count]
+                if held and i in parts_of(step, m):
+                    if (step, m, i) not in seen:
+                        seen.add((step, m, i))
+                        bc[step, m, i].wait_recv()
+                    for n in held:
+                        more = brecv[dst + n, sub(0, 1, i)[1]].astype(F32)
+                        values[src + n - first] = values[src + n - first] + more
+        return values
+
+    def send_back(step):
         for i in range(PARTS):
-            for r in distances:
-                n = SLOT[r]
-                bsend[sub(n, i)] = summed(r, i)
-                bc[r, i] = send(
-                    bsend.at[sub(n, i)], brecv.at[sub(n, i)],
-                    b_s.at[n, i], b_r.at[n, i], zs[sources(r, i)[0]],
-                )
-
-    send_back(8, -3, 3)
+            for m, (_, dst, count, far) in enumerate(STEPS[step]):
+                if i in parts_of(step, m):
+                    for n, value in enumerate(summed(dst, count, i)):
+                        bsend[dst + n, sub(0, 1, i)[1]] = value.astype(BF16)
+                    bc[step, m, i] = send(
+                        bsend.at[sub(dst, count, i)], brecv.at[sub(dst, count, i)],
+                        b_s.at[dst, i], b_r.at[dst, i], zs[-far],
+                    )
+
+    send_back(3)
+    send_back(2)
     sum_by_topic(0)
-    send_back(-7, 7)
-    send_back(-4, 4, -2, 2, -6, 6)
-    paced(send_rs, RS_PACE, 2)
-    send_back(-5, 5, -1, 1)
+    send_rs(0, 2)
+    send_rs(1, 2)
+    send_back(1)
+    send_back(0)
     fin_c = []
     for i in range(PARTS):
-        fin[sub(x, i)] = summed(0, i)
+        rows = sub(0, 1, i)[1]
+        value = table[0, rows]
+        for m, (_, dst, _, _) in enumerate(STEPS[0]):
+            bc[0, m, i].wait_recv()
+            value = value + brecv[dst, rows].astype(F32)
+        fin[x, rows] = value.astype(BF16)
         for o in range(1, NX):
-            rows = fin.at[sub(x, i)]
-            fin_c.append(send(rows, rows, fin_s.at[o - 1, i], fin_r.at[o - 1, i], xs[o]))
+            here = fin.at[x, rows]
+            fin_c.append(send(here, here, fin_s.at[o - 1, i], fin_r.at[o - 1, i], xs[o]))
     query_part(0)
     got(rs, *((way, n) for n in range(PIECES, 3 * PIECES) for way in range(2)))
     for half in range(2):

time: 87.1 us -> 86.2 us (0.990)
  the two profiles are of different devices: /device:TPU:2 before, /device:TPU:4 now
where the time goes in v3:
time: 86.2 us; the launch traced here: 86.1 us
  Pallas kernels  81.6 us (95%)
  local copies, waits for them, and re-layouts  3.84 us (4%)
    pallas_call x1, Pallas kernels, shards(): pl.pallas_call(kernel, out_shape=(jax.ShapeDtypeStruct((2, 128), F32), ja...  81.6 us
    unnamed x7, local copies, waits for them, and re-layouts  3.84 us

profile of v3, /device:TPU:4, one launch (start us, length us, event | category | flops | bytes accessed | tf_op | source)
XLA Modules:
  0.0 86.1 jit_solution(10441125133316632638)
XLA Ops:
  0.6 81.6 %shard_map.76 = (f32[2,128]{1,0:T(2,128)}, bf16[256,1024]{1,0:T(8,128)(2,1)}, bf16[128,1024]{1,0:T(8,128)(2,1)}) custom-call(bf16[256,1024]{1,0:T(8,128)(2,1)} %q_ref.1, bf16[128,1024]{1,0:T(8,128)(2,1)} %p_ref.1, s32[128]{0:T(128)} %gt_ref.1, s32[16,1024]{1,0:T(8,128)} %rows_ref.1, s32[1,256]{1,0:T(1,128)} %bitcast.3), custom_call_target="tpu_custom_call" | custom-call | flops 1610612736 | bytes 2097152 | tf_op jit(solution)/shard_map/pallas_call | solution.py:398
  82.2 0.0 copy-start.1
  82.2 0.7 copy-done.1
  82.9 0.6 copy.11
  83.4 0.0 copy-start
  83.4 1.9 %copy.12 = bf16[256,1024]{1,0:T(8,128)(2,1)} copy(bf16[256,1024]{1,0:T(8,128)(2,1)} %get-tuple-element.13) | data formatting | bytes 1048576
  85.4 0.0 copy-done
  85.4 0.7 copy.13
Async XLA Ops:
  82.2 0.7 copy-start.1
  83.4 1.9 %copy-start = (bf16[128,1024]{1,0:T(8,128)(2,1)S(1)}, bf16[128,1024]{1,0:T(8,128)(2,1)}, u32[]{:S(2)}) copy-start(bf16[128,1024]{1,0:T(8,128)(2,1)} %get-tuple-element.14) | copy-start | bytes 786436

commit v4 on v3

--- a/solution.py
+++ b/solution.py
@@ -16,7 +16,7 @@
 BLOCK = SHARE * TOPICS
 HALF = 128
 PARTS = 2
-Q_PACE = (1, 1, 1)
+Q_PACE = (2, 1)
 PIECES, PIECE = 1, 128
 
 ORDER = (0, -1, -5, 5, 1, -2, -6, 4, -4, 6, 2, -7, 3, -3, 7, 8)
@@ -184,7 +184,6 @@
         for o in range(1, NX)
     ]
     receive(1)
-    paced(send_q, Q_PACE, 2)
     pick(0)
     receive(2)
     receive(3)
@@ -311,11 +310,11 @@
             )
 
     weigh(1)
-    term(1)
     weigh(0)
     query_part(2)
     send_rs(0, 0)
     send_rs(1, 0)
+    term(1)
     query_part(1)
     send_rs(0, 1)
     query_part(3)

time: 86.2 us -> 87.3 us (1.013)
  Pallas kernels: 81.6 us -> 82.6 us
    pallas_call x1, Pallas kernels: 81.6 us -> 82.6 us  [shards(): pl.pallas_call(kernel, out_shape=(jax.ShapeDtypeStruct((2, 128), F32), ja...]
where the time goes in v4:
time: 87.3 us; the launch traced here: 87.1 us
  Pallas kernels  82.6 us (95%)
  local copies, waits for them, and re-layouts  3.84 us (4%)
    pallas_call x1, Pallas kernels, shards(): pl.pallas_call(kernel, out_shape=(jax.ShapeDtypeStruct((2, 128), F32), ja...  82.6 us
    unnamed x7, local copies, waits for them, and re-layouts  3.84 us

profile of v4, /device:TPU:4, one launch (start us, length us, event | category | flops | bytes accessed | tf_op | source)
XLA Modules:
  0.0 87.1 jit_solution(12941371289248755126)
XLA Ops:
  0.6 82.6 %shard_map.76 = (f32[2,128]{1,0:T(2,128)}, bf16[256,1024]{1,0:T(8,128)(2,1)}, bf16[128,1024]{1,0:T(8,128)(2,1)}) custom-call(bf16[256,1024]{1,0:T(8,128)(2,1)} %q_ref.1, bf16[128,1024]{1,0:T(8,128)(2,1)} %p_ref.1, s32[128]{0:T(128)} %gt_ref.1, s32[16,1024]{1,0:T(8,128)} %rows_ref.1, s32[1,256]{1,0:T(1,128)} %bitcast.3), custom_call_target="tpu_custom_call" | custom-call | flops 1610612736 | bytes 2097152 | tf_op jit(solution)/shard_map/pallas_call | solution.py:397
  83.3 0.0 copy-start.1
  83.3 0.7 copy-done.1
  83.9 0.6 copy.11
  84.5 0.0 copy-start
  84.5 1.9 %copy.12 = bf16[256,1024]{1,0:T(8,128)(2,1)} copy(bf16[256,1024]{1,0:T(8,128)(2,1)} %get-tuple-element.13) | data formatting | bytes 1048576
  86.4 0.0 copy-done
  86.4 0.7 copy.13
Async XLA Ops:
  83.3 0.7 copy-start.1
  84.5 1.9 %copy-start = (bf16[128,1024]{1,0:T(8,128)(2,1)S(1)}, bf16[128,1024]{1,0:T(8,128)(2,1)}, u32[]{:S(2)}) copy-start(bf16[128,1024]{1,0:T(8,128)(2,1)} %get-tuple-element.14) | copy-start | bytes 786436

commit v5 on v3

--- a/solution.py
+++ b/solution.py
@@ -15,6 +15,7 @@
 SHARE = 2
 BLOCK = SHARE * TOPICS
 HALF = 128
+FAR_FIRST = (4, 3, 5, 2, 6, 1, 7)
 PARTS = 2
 Q_PACE = (1, 1, 1)
 PIECES, PIECE = 1, 128
@@ -96,10 +97,12 @@
     first = (dp % 16) * 8
     loads[0].wait()
     here = rows_here[...] - dp * OWN
-    for i in range(8):
+
+    def where_listed(i):
         col = jnp.sum(jnp.where(lane == first + i, here, 0).astype(F32), axis=1, keepdims=True)
-        mat[i * 16 : (i + 1) * 16, :] = jnp.where(lane.astype(F32) == col, 1.0, 0.0).astype(BF16)
-    mine = mat[pl.ds(pl.multiple_of(x * BLOCK, BLOCK), BLOCK), :]
+        return jnp.where(lane.astype(F32) == col, 1.0, 0.0).astype(BF16)
+
+    mine = jnp.concatenate([where_listed(x * SHARE + i) for i in range(SHARE)], axis=0)
     loads[1].wait()
     zbuf[0] = dot(mine, pass_here[...]).astype(BF16)
     for load in loads[2:]:
@@ -155,6 +158,8 @@
         chosen = at + topics[z * NE + d]
         smat[d * 16 : (d + 1) * 16, :] = jnp.where(c256 == chosen, 1.0, 0.0).astype(BF16)
     smat_t[...] = smat[...].T
+    for i in range(8):
+        mat[i * 16 : (i + 1) * 16, :] = where_listed(i)
     mat_t[...] = mat[...].T
 
     yc = {}
@@ -162,7 +167,7 @@
     def pick(ch):
         blocks = zbuf[ch * 8 : (ch + 1) * 8].reshape(256, D)
         ysend[ch] = dot(smat[...], blocks).astype(BF16).reshape(NE, 16, D)
-        for o in range(1, NE):
+        for o in FAR_FIRST:
             yc[ch, o] = send(
                 ysend.at[ch, e_at[o]], picked.at[ch, e],
                 y_s.at[ch, o - 1], y_r.at[ch, o - 1], es[o],
@@ -278,7 +283,7 @@
             return 0
 
         lax.fori_loop(0, D // 256, tile, 0)
-        for o in range(1, NE):
+        for o in FAR_FIRST:
             gc[ch, o] = send(
                 gsend.at[ch, e_at[o]], grecv.at[ch, e],
                 g_s.at[ch, o - 1], g_r.at[ch, o - 1], es[o],

time: 86.2 us -> 87 us (level)
  the two profiles are of different devices: /device:TPU:4 before, /device:TPU:8 now
where the time goes in v5:
time: 87 us; the launch traced here: 86.8 us
  Pallas kernels  82.3 us (95%)
  local copies, waits for them, and re-layouts  3.84 us (4%)
    pallas_call x1, Pallas kernels, shards(): pl.pallas_call(kernel, out_shape=(jax.ShapeDtypeStruct((2, 128), F32), ja...  82.3 us
    unnamed x7, local copies, waits for them, and re-layouts  3.84 us

profile of v5, /device:TPU:8, one launch (start us, length us, event | category | flops | bytes accessed | tf_op | source)
XLA Modules:
  0.0 86.8 jit_solution(12741794879748578743)
XLA Ops:
  0.6 82.3 %shard_map.76 = (f32[2,128]{1,0:T(2,128)}, bf16[256,1024]{1,0:T(8,128)(2,1)}, bf16[128,1024]{1,0:T(8,128)(2,1)}) custom-call(bf16[256,1024]{1,0:T(8,128)(2,1)} %q_ref.1, bf16[128,1024]{1,0:T(8,128)(2,1)} %p_ref.1, s32[128]{0:T(128)} %gt_ref.1, s32[16,1024]{1,0:T(8,128)} %rows_ref.1, s32[1,256]{1,0:T(1,128)} %bitcast.3), custom_call_target="tpu_custom_call" | custom-call | flops 1610612736 | bytes 2097152 | tf_op jit(solution)/shard_map/pallas_call | solution.py:403
  82.9 0.0 copy-start.1
  83.0 0.7 copy-done.1
  83.6 0.6 copy.11
  84.2 0.0 copy-start
  84.2 1.9 %copy.12 = bf16[256,1024]{1,0:T(8,128)(2,1)} copy(bf16[256,1024]{1,0:T(8,128)(2,1)} %get-tuple-element.13) | data formatting | bytes 1048576
  86.1 0.0 copy-done
  86.1 0.7 copy.13
Async XLA Ops:
  82.9 0.7 copy-start.1
  84.2 1.9 %copy-start = (bf16[128,1024]{1,0:T(8,128)(2,1)S(1)}, bf16[128,1024]{1,0:T(8,128)(2,1)}, u32[]{:S(2)}) copy-start(bf16[128,1024]{1,0:T(8,128)(2,1)} %get-tuple-element.14) | copy-start | bytes 786436

commit v6 on v3

--- a/solution.py
+++ b/solution.py
@@ -359,9 +359,9 @@
     send_back(3)
     send_back(2)
     sum_by_topic(0)
+    send_back(1)
     send_rs(0, 2)
     send_rs(1, 2)
-    send_back(1)
     send_back(0)
     fin_c = []
     for i in range(PARTS):

time: 86.2 us -> 86 us (level)
  the two profiles are of different devices: /device:TPU:4 before, /device:TPU:16 now
where the time goes in v6:
time: 86 us; the launch traced here: 85.9 us
  Pallas kernels  81.4 us (95%)
  local copies, waits for them, and re-layouts  3.84 us (4%)
    pallas_call x1, Pallas kernels, shards(): pl.pallas_call(kernel, out_shape=(jax.ShapeDtypeStruct((2, 128), F32), ja...  81.4 us
    unnamed x7, local copies, waits for them, and re-layouts  3.84 us

profile of v6, /device:TPU:16, one launch (start us, length us, event | category | flops | bytes accessed | tf_op | source)
XLA Modules:
  0.0 85.9 jit_solution(3931461756275819100)
XLA Ops:
  0.6 81.4 %shard_map.76 = (f32[2,128]{1,0:T(2,128)}, bf16[256,1024]{1,0:T(8,128)(2,1)}, bf16[128,1024]{1,0:T(8,128)(2,1)}) custom-call(bf16[256,1024]{1,0:T(8,128)(2,1)} %q_ref.1, bf16[128,1024]{1,0:T(8,128)(2,1)} %p_ref.1, s32[128]{0:T(128)} %gt_ref.1, s32[16,1024]{1,0:T(8,128)} %rows_ref.1, s32[1,256]{1,0:T(1,128)} %bitcast.3), custom_call_target="tpu_custom_call" | custom-call | flops 1610612736 | bytes 2097152 | tf_op jit(solution)/shard_map/pallas_call | solution.py:398
  82.0 0.0 copy-start.1
  82.0 0.7 copy-done.1
  82.7 0.6 copy.11
  83.2 0.0 copy-start
  83.2 1.9 %copy.12 = bf16[256,1024]{1,0:T(8,128)(2,1)} copy(bf16[256,1024]{1,0:T(8,128)(2,1)} %get-tuple-element.13) | data formatting | bytes 1048576
  85.2 0.0 copy-done
  85.2 0.7 copy.13
Async XLA Ops:
  82.0 0.7 copy-start.1
  83.2 1.9 %copy-start = (bf16[128,1024]{1,0:T(8,128)(2,1)S(1)}, bf16[128,1024]{1,0:T(8,128)(2,1)}, u32[]{:S(2)}) copy-start(bf16[128,1024]{1,0:T(8,128)(2,1)} %get-tuple-element.14) | copy-start | bytes 786436
